TPU v7x, 256 devices: a whole 4x4x8 slice. The times are simulated.
256 devices in a mesh: seq: 32 (over z_hi, y, core), head: 8 (over z_lo, x).
Axes of the slice: x: 4, y: 4, z: 8 (z_hi: 4, z_lo: 2; z = z_hi * 2 + z_lo), core: 2. Of those that a mesh axis runs over, the one named last changes fastest.
Arguments:
- queries: bfloat16 [32768, 6144], P(('seq', 'head')), may hold values from -8 to 8
- keys: bfloat16 [32768, 6144], P(('seq', 'head')), may hold values from -8 to 8
- values: bfloat16 [32768, 6144], P(('seq', 'head')), may hold values from -15 to 15
- block_lists: int32 [256, 20], P('seq'), may hold values from 0 to 255, as said below
- live_counts: int32 [256], P('seq'), may hold values from 10 to 20, as said below
Outputs:
- attended: bfloat16 [32768, 6144], P(('seq', 'head'))
Inputs may be any that keep to these rules, and one draw needn't show every extreme that they name: `block_lists`: slot 0 of row b is b itself; a row's blocks are distinct. With the band of block g being g // 8 and its place p = g % 8, a query block of band t names only blocks of bands t - 2 to t + 2 taken modulo the number of bands; of band t - 2 only places p >= 4, of band t + 2 only places p < 4. `live_counts`: the first query block of every latitude band has 20.
All inputs are finite; a program needn't handle non-finite values.
Results may differ from a plain program's by a relative error of at most 0.0037.
Values may be sent and summed in bfloat16 or wider, within the bound.
A program may use at most 128 MiB of HBM per device.

v0:
```python
import jax
import jax.numpy as jnp
from jax import lax
from jax.sharding import PartitionSpec as P

HD = 128
BLK = 128


def from_behind(block, axis, distance):
    devices = range(lax.axis_size(axis))
    route = [((i - distance) % len(devices), i) for i in devices]
    return lax.ppermute(block, axis, route)


def attend_heads(query_heads, key_heads, value_heads, live_count, block_rows, head_size):
    scores = jnp.einsum(
        "hqd,hkd->hqk", query_heads, key_heads, preferred_element_type=jnp.float32
    ) * head_size ** (-0.5)
    is_valid = jnp.arange(key_heads.shape[1], dtype=jnp.int32) // block_rows < live_count
    scores = jnp.where(is_valid[None, None, :], scores, jnp.float32(-1e30))
    row_max = jnp.max(scores, axis=-1, keepdims=True)
    expo = jnp.where(is_valid[None, None, :], jnp.exp(scores - row_max), jnp.float32(0.0))
    row_total = jnp.sum(expo, axis=-1, keepdims=True)
    weights = expo.astype(jnp.bfloat16)
    summed = jnp.einsum("hqk,hkd->hqd", weights, value_heads, preferred_element_type=jnp.float32)
    return (summed / row_total).astype(jnp.bfloat16)


def local(queries, keys, values, block_lists, live_counts):
    local_queries, local_keys, local_values = (
        lax.all_to_all(queries, "head", split_axis=1, concat_axis=0, tiled=True),
        lax.all_to_all(keys, "head", split_axis=1, concat_axis=0, tiled=True),
        lax.all_to_all(values, "head", split_axis=1, concat_axis=0, tiled=True),
    )
    band_tokens = local_queries.shape[0]
    group_width = local_queries.shape[1]
    blocks_dev = band_tokens // BLK
    head_count = group_width // HD
    query_major = jnp.transpose(local_queries.reshape(band_tokens, head_count, HD), (1, 0, 2))
    stacked = jnp.stack((local_keys, local_values)).reshape(2, band_tokens, head_count, HD)
    stacked = jnp.transpose(stacked, (0, 2, 1, 3))
    pieces = {}
    for hops in (2, 1, -1, -2):
        pieces[hops] = from_behind(stacked, "seq", hops)
    key_band = jnp.concatenate([pieces[2], pieces[1], stacked, pieces[-1], pieces[-2]], axis=2)
    own_start = 2 * blocks_dev
    my_band = lax.axis_index("seq")
    band_count = lax.axis_size("seq")
    owner_band = block_lists // blocks_dev
    within = block_lists % blocks_dev
    offset = (owner_band - my_band) % band_count
    offset = jnp.where(offset > band_count // 2, offset - band_count, offset)
    positions = own_start + offset * blocks_dev + within
    band_blocks = key_band.reshape(2, head_count, key_band.shape[2] // BLK, BLK, HD)

    def one_block(block_index):
        query_heads = lax.dynamic_slice_in_dim(query_major, block_index * BLK, BLK, 1)
        picked = band_blocks[:, :, positions[block_index]]
        picked = picked.reshape(2, head_count, -1, HD)
        return attend_heads(query_heads, picked[0], picked[1], live_counts[block_index], BLK, HD)

    outputs = lax.map(one_block, jnp.arange(blocks_dev, dtype=jnp.int32))
    outputs = jnp.transpose(outputs, (0, 2, 1, 3)).reshape(band_tokens, group_width)
    return lax.all_to_all(outputs, "head", split_axis=0, concat_axis=1, tiled=True)


def solution(mesh):
    in_specs = (
        P(("seq", "head"), None),
        P(("seq", "head"), None),
        P(("seq", "head"), None),
        P("seq", None),
        P("seq"),
    )
    out_specs = P(("seq", "head"), None)
    return jax.shard_map(local, mesh=mesh, in_specs=in_specs, out_specs=out_specs, check_vma=False)
```

profile of v0, /device:TPU:89, one launch (start us, length us, event | category | flops | bytes accessed | tf_op | source)
XLA Modules:
  0.0 623.6 jit_solution(3227277688074203394)
XLA Ops:
  0.0 2.7 copy.23
  2.7 5.4 all-to-all-start.2
  9.7 18.9 %all-to-all-done.2 = bf16[128,8,768]{0,2,1:T(8,128)(2,1)S(1)} async-done(((bf16[128,8,768]{0,2,1:T(8,128)(2,1)}), bf16[128,8,768]{0,2,1:T(8,128)(2,1)S(1)}, u32[]{:S(2)}, u32[]{:S(2)}) %all-to-all-start.2) | async-done | bytes 1572896 | tf_op jit(solution)/shard_map/all_to_all | solution.py:34
  28.6 3.7 all-to-all-start.1
  37.0 15.8 %all-to-all-done.1 = bf16[128,8,768]{0,2,1:T(8,128)(2,1)S(1)} async-done(((bf16[128,8,768]{0,2,1:T(8,128)(2,1)}), bf16[128,8,768]{0,2,1:T(8,128)(2,1)S(1)}, u32[]{:S(2)}, u32[]{:S(2)}) %all-to-all-start.1) | async-done | bytes 1572896 | tf_op jit(solution)/shard_map/all_to_all | solution.py:33
  59.5 3.0 collective-permute-start
  64.7 2.6 copy.19
  67.3 4.3 all-to-all-start
  72.1 210.1 %all-to-all-done = bf16[128,8,768]{0,2,1:T(8,128)(2,1)} async-done(((bf16[128,8,768]{0,2,1:T(8,128)(2,1)}), bf16[128,8,768]{0,2,1:T(8,128)(2,1)}, u32[]{:S(2)}, u32[]{:S(2)}) %all-to-all-start) | async-done | bytes 1572896 | tf_op jit(solution)/shard_map/all_to_all | solution.py:32
  282.3 3.6 copy.20
  285.8 3.7 reshape.84
  289.6 4.0 constant_dynamic-update-slice_fusion.5
  293.6 4.0 constant_dynamic-update-slice_fusion.4
  300.0 4.0 constant_dynamic-update-slice_fusion.2
  304.0 4.0 constant_dynamic-update-slice_fusion.1
  308.0 20.8 %copy.29 = bf16[2,6,5120,128]{3,2,1,0:T(8,128)(2,1)} copy(bf16[2,6,5120,128]{2,3,1,0:T(8,128)(2,1)} %constant_dynamic-update-slice_fusion.1) | data formatting | bytes 31457280 | tf_op jit(solution)/shard_map/while | solution.py:63
  328.7 276.1 %while.12 = (s32[]{:T(128)}, bf16[8,6,128,128]{2,3,1,0:T(8,128)(2,1)S(1)}, s32[8]{0:T(128)S(1)}, s32[8]{0:T(128)S(1)}, bf16[6,1024,128]{1,2,0:T(8,128)(2,1)}, /*...) while((s32[]{:T(128)}, ...), condition=%wide.region_3.4_spmd, body=%wide.region_0.3_spmd.sunk | while | flops 1018652736 | bytes 79842376 | solution.py:63
  332.0 10.8 %gather_fusion = bf16[20,2,6,128,128]{4,3,2,1,0:T(8,128)(2,1)} fusion(bf16[2,6,40,128,128]{4,3,2,1,0:T(8,128)(2,1)} %get-tuple-element.211, s32[1024]{0:T(1024)S(1)} %pad_clamp_fusion.2), kind=kCustom, calls=%fused_computation.clone.1 | custom fusion | bytes 15728720 | tf_op jit(solution)/shard_map/while/body/eval_jaxpr/gather | solution.py:59
  342.8 5.0 fusion.62
  351.3 7.3 %fusion.64 = (f32[6,128]{1,0:T(8,128)S(1)}, bf16[6,128,2560]{2,1,0:T(8,128)(2,1)}) fusion(pred[2560]{0:T(1024)(128)(4,1)S(1)} %fusion.63, bf16[6,2560,128]{2,1,0:T(8,128)(2,1)} %bitcast.66, bf16[6,1024,128]{1,2,0:T(8,128)(2,1)} %get-tuple-element.209, s32[]{:T(128)S(6)} %select_n.122), kind=kOutput, calls=%fused_computation.58.clone.1 | convolution fusion | flops 515115520 | bytes 8070148 | tf_op jit(solution)/shard_map/while/body/eval_jaxpr/sub | solution.py:23
  358.6 2.6 copy.36
  366.5 10.8 %gather_fusion = bf16[20,2,6,128,128]{4,3,2,1,0:T(8,128)(2,1)} fusion(bf16[2,6,40,128,128]{4,3,2,1,0:T(8,128)(2,1)} %get-tuple-element.211, s32[1024]{0:T(1024)S(1)} %pad_clamp_fusion.2), kind=kCustom, calls=%fused_computation.clone.1 | custom fusion | bytes 15728720 | tf_op jit(solution)/shard_map/while/body/eval_jaxpr/gather | solution.py:59
  377.3 5.0 fusion.62
  385.8 7.3 %fusion.64 = (f32[6,128]{1,0:T(8,128)S(1)}, bf16[6,128,2560]{2,1,0:T(8,128)(2,1)}) fusion(pred[2560]{0:T(1024)(128)(4,1)S(1)} %fusion.63, bf16[6,2560,128]{2,1,0:T(8,128)(2,1)} %bitcast.66, bf16[6,1024,128]{1,2,0:T(8,128)(2,1)} %get-tuple-element.209, s32[]{:T(128)S(6)} %select_n.122), kind=kOutput, calls=%fused_computation.58.clone.1 | convolution fusion | flops 515115520 | bytes 8070148 | tf_op jit(solution)/shard_map/while/body/eval_jaxpr/sub | solution.py:23
  393.1 2.6 copy.36
  401.0 10.8 %gather_fusion = bf16[20,2,6,128,128]{4,3,2,1,0:T(8,128)(2,1)} fusion(bf16[2,6,40,128,128]{4,3,2,1,0:T(8,128)(2,1)} %get-tuple-element.211, s32[1024]{0:T(1024)S(1)} %pad_clamp_fusion.2), kind=kCustom, calls=%fused_computation.clone.1 | custom fusion | bytes 15728720 | tf_op jit(solution)/shard_map/while/body/eval_jaxpr/gather | solution.py:59
  411.8 5.0 fusion.62
  420.3 7.3 %fusion.64 = (f32[6,128]{1,0:T(8,128)S(1)}, bf16[6,128,2560]{2,1,0:T(8,128)(2,1)}) fusion(pred[2560]{0:T(1024)(128)(4,1)S(1)} %fusion.63, bf16[6,2560,128]{2,1,0:T(8,128)(2,1)} %bitcast.66, bf16[6,1024,128]{1,2,0:T(8,128)(2,1)} %get-tuple-element.209, s32[]{:T(128)S(6)} %select_n.122), kind=kOutput, calls=%fused_computation.58.clone.1 | convolution fusion | flops 515115520 | bytes 8070148 | tf_op jit(solution)/shard_map/while/body/eval_jaxpr/sub | solution.py:23
  435.5 10.8 %gather_fusion = bf16[20,2,6,128,128]{4,3,2,1,0:T(8,128)(2,1)} fusion(bf16[2,6,40,128,128]{4,3,2,1,0:T(8,128)(2,1)} %get-tuple-element.211, s32[1024]{0:T(1024)S(1)} %pad_clamp_fusion.2), kind=kCustom, calls=%fused_computation.clone.1 | custom fusion | bytes 15728720 | tf_op jit(solution)/shard_map/while/body/eval_jaxpr/gather | solution.py:59
  446.3 5.0 fusion.62
  454.8 7.3 %fusion.64 = (f32[6,128]{1,0:T(8,128)S(1)}, bf16[6,128,2560]{2,1,0:T(8,128)(2,1)}) fusion(pred[2560]{0:T(1024)(128)(4,1)S(1)} %fusion.63, bf16[6,2560,128]{2,1,0:T(8,128)(2,1)} %bitcast.66, bf16[6,1024,128]{1,2,0:T(8,128)(2,1)} %get-tuple-element.209, s32[]{:T(128)S(6)} %select_n.122), kind=kOutput, calls=%fused_computation.58.clone.1 | convolution fusion | flops 515115520 | bytes 8070148 | tf_op jit(solution)/shard_map/while/body/eval_jaxpr/sub | solution.py:23
  462.1 2.6 copy.36
  470.0 10.8 %gather_fusion = bf16[20,2,6,128,128]{4,3,2,1,0:T(8,128)(2,1)} fusion(bf16[2,6,40,128,128]{4,3,2,1,0:T(8,128)(2,1)} %get-tuple-element.211, s32[1024]{0:T(1024)S(1)} %pad_clamp_fusion.2), kind=kCustom, calls=%fused_computation.clone.1 | custom fusion | bytes 15728720 | tf_op jit(solution)/shard_map/while/body/eval_jaxpr/gather | solution.py:59
  480.8 5.0 fusion.62
  489.3 7.3 %fusion.64 = (f32[6,128]{1,0:T(8,128)S(1)}, bf16[6,128,2560]{2,1,0:T(8,128)(2,1)}) fusion(pred[2560]{0:T(1024)(128)(4,1)S(1)} %fusion.63, bf16[6,2560,128]{2,1,0:T(8,128)(2,1)} %bitcast.66, bf16[6,1024,128]{1,2,0:T(8,128)(2,1)} %get-tuple-element.209, s32[]{:T(128)S(6)} %select_n.122), kind=kOutput, calls=%fused_computation.58.clone.1 | convolution fusion | flops 515115520 | bytes 8070148 | tf_op jit(solution)/shard_map/while/body/eval_jaxpr/sub | solution.py:23
  496.6 2.6 copy.36
  504.5 10.8 %gather_fusion = bf16[20,2,6,128,128]{4,3,2,1,0:T(8,128)(2,1)} fusion(bf16[2,6,40,128,128]{4,3,2,1,0:T(8,128)(2,1)} %get-tuple-element.211, s32[1024]{0:T(1024)S(1)} %pad_clamp_fusion.2), kind=kCustom, calls=%fused_computation.clone.1 | custom fusion | bytes 15728720 | tf_op jit(solution)/shard_map/while/body/eval_jaxpr/gather | solution.py:59
  515.3 5.0 fusion.62
  523.8 7.3 %fusion.64 = (f32[6,128]{1,0:T(8,128)S(1)}, bf16[6,128,2560]{2,1,0:T(8,128)(2,1)}) fusion(pred[2560]{0:T(1024)(128)(4,1)S(1)} %fusion.63, bf16[6,2560,128]{2,1,0:T(8,128)(2,1)} %bitcast.66, bf16[6,1024,128]{1,2,0:T(8,128)(2,1)} %get-tuple-element.209, s32[]{:T(128)S(6)} %select_n.122), kind=kOutput, calls=%fused_computation.58.clone.1 | convolution fusion | flops 515115520 | bytes 8070148 | tf_op jit(solution)/shard_map/while/body/eval_jaxpr/sub | solution.py:23
  531.1 2.6 copy.36
  539.0 10.8 %gather_fusion = bf16[20,2,6,128,128]{4,3,2,1,0:T(8,128)(2,1)} fusion(bf16[2,6,40,128,128]{4,3,2,1,0:T(8,128)(2,1)} %get-tuple-element.211, s32[1024]{0:T(1024)S(1)} %pad_clamp_fusion.2), kind=kCustom, calls=%fused_computation.clone.1 | custom fusion | bytes 15728720 | tf_op jit(solution)/shard_map/while/body/eval_jaxpr/gather | solution.py:59
  549.8 5.0 fusion.62
  558.3 7.3 %fusion.64 = (f32[6,128]{1,0:T(8,128)S(1)}, bf16[6,128,2560]{2,1,0:T(8,128)(2,1)}) fusion(pred[2560]{0:T(1024)(128)(4,1)S(1)} %fusion.63, bf16[6,2560,128]{2,1,0:T(8,128)(2,1)} %bitcast.66, bf16[6,1024,128]{1,2,0:T(8,128)(2,1)} %get-tuple-element.209, s32[]{:T(128)S(6)} %select_n.122), kind=kOutput, calls=%fused_computation.58.clone.1 | convolution fusion | flops 515115520 | bytes 8070148 | tf_op jit(solution)/shard_map/while/body/eval_jaxpr/sub | solution.py:23
  565.6 2.6 copy.36
  573.5 10.8 %gather_fusion = bf16[20,2,6,128,128]{4,3,2,1,0:T(8,128)(2,1)} fusion(bf16[2,6,40,128,128]{4,3,2,1,0:T(8,128)(2,1)} %get-tuple-element.211, s32[1024]{0:T(1024)S(1)} %pad_clamp_fusion.2), kind=kCustom, calls=%fused_computation.clone.1 | custom fusion | bytes 15728720 | tf_op jit(solution)/shard_map/while/body/eval_jaxpr/gather | solution.py:59
  584.3 5.0 fusion.62
  592.8 7.3 %fusion.64 = (f32[6,128]{1,0:T(8,128)S(1)}, bf16[6,128,2560]{2,1,0:T(8,128)(2,1)}) fusion(pred[2560]{0:T(1024)(128)(4,1)S(1)} %fusion.63, bf16[6,2560,128]{2,1,0:T(8,128)(2,1)} %bitcast.66, bf16[6,1024,128]{1,2,0:T(8,128)(2,1)} %get-tuple-element.209, s32[]{:T(128)S(6)} %select_n.122), kind=kOutput, calls=%fused_computation.58.clone.1 | convolution fusion | flops 515115520 | bytes 8070148 | tf_op jit(solution)/shard_map/while/body/eval_jaxpr/sub | solution.py:23
  604.8 17.2 %all_to_all.67 = bf16[8,128,768]{1,2,0:T(8,128)(2,1)S(1)} all-to-all(bf16[8,128,768]{1,2,0:T(8,128)(2,1)S(1)} %bitcast.73), channel_id=1, replica_groups=mesh['seq'=32,'head'=8] {'head'}, dimensions={0} | all-to-all | bytes 3145728 | tf_op jit(solution)/shard_map/all_to_all | solution.py:65
  (116 shorter events, 74.2 us)
Async XLA Ops:
  0.0 8.1 %copy-start = (bf16[128,6144]{1,0:T(8,128)(2,1)S(1)}, bf16[128,6144]{1,0:T(8,128)(2,1)}, u32[]{:S(2)}) copy-start(bf16[128,6144]{1,0:T(8,128)(2,1)} %param.8) | copy-start | bytes 4718596
  2.7 25.9 %all-to-all-start.2 = ((bf16[128,8,768]{0,2,1:T(8,128)(2,1)}), bf16[128,8,768]{0,2,1:T(8,128)(2,1)S(1)}, u32[]{:S(2)}, u32[]{:S(2)}) async-start(bf16[128,8,768]{0,2,1:T(8,128)(2,1)} %bitcast.13), calls=%async_computation.2 | async-start | bytes 3145728 | tf_op jit(solution)/shard_map/all_to_all | solution.py:34
  28.6 24.3 %all-to-all-start.1 = ((bf16[128,8,768]{0,2,1:T(8,128)(2,1)}), bf16[128,8,768]{0,2,1:T(8,128)(2,1)S(1)}, u32[]{:S(2)}, u32[]{:S(2)}) async-start(bf16[128,8,768]{0,2,1:T(8,128)(2,1)} %bitcast.11), calls=%async_computation.1 | async-start | bytes 3145728 | tf_op jit(solution)/shard_map/all_to_all | solution.py:33
  59.5 12.7 %copy-start.2 = (s32[8,20]{1,0:T(8,128)S(1)}, s32[8,20]{1,0:T(8,128)}, u32[]{:S(2)}) copy-start(s32[8,20]{1,0:T(8,128)} %param.10) | copy-start | bytes 1924
  59.5 230.1 %collective-permute-start = (bf16[2,6,1024,128]{2,3,1,0:T(8,128)(2,1)}, bf16[2,6,1024,128]{2,3,1,0:T(8,128)(2,1)}, u32[]{:S(2)}, u32[]{:S(2)}) collective-permute-start(bf16[2,6,1024,128]{2,3,1,0:T(8,128)(2,1)} %maximum_bitcast_fusion), channel_id=1, source_target_pairs={{240,0},{248,8},{0,16},{8,24},{16,32},{24,40},{32,48},{40,56},{48,... | collective-permute-start | bytes 9437192 | tf_op jit(solution)/shard_map/ppermute | solution.py:13
  62.4 231.2 %collective-permute-start.1 = (bf16[2,6,1024,128]{2,3,1,0:T(8,128)(2,1)}, bf16[2,6,1024,128]{2,3,1,0:T(8,128)(2,1)}, u32[]{:S(2)}, u32[]{:S(2)}) collective-permute-start(bf16[2,6,1024,128]{2,3,1,0:T(8,128)(2,1)} %maximum_bitcast_fusion), channel_id=1, source_target_pairs={{248,0},{0,8},{8,16},{16,24},{24,32},{32,40},{40,48},{48,56},{56,6... | collective-permute-start | bytes 9437192 | tf_op jit(solution)/shard_map/ppermute | solution.py:13
  67.3 215.0 %all-to-all-start = ((bf16[128,8,768]{0,2,1:T(8,128)(2,1)}), bf16[128,8,768]{0,2,1:T(8,128)(2,1)}, u32[]{:S(2)}, u32[]{:S(2)}) async-start(bf16[128,8,768]{0,2,1:T(8,128)(2,1)} %bitcast.68), calls=%async_computation | async-start | bytes 3145728 | tf_op jit(solution)/shard_map/all_to_all | solution.py:32
  71.6 228.4 %collective-permute-start.2 = (bf16[2,6,1024,128]{2,3,1,0:T(8,128)(2,1)}, bf16[2,6,1024,128]{2,3,1,0:T(8,128)(2,1)}, u32[]{:S(2)}, u32[]{:S(2)}) collective-permute-start(bf16[2,6,1024,128]{2,3,1,0:T(8,128)(2,1)} %maximum_bitcast_fusion), channel_id=1, source_target_pairs={{8,0},{16,8},{24,16},{32,24},{40,32},{48,40},{56,48},{64,56},{72,6... | collective-permute-start | bytes 9437192 | tf_op jit(solution)/shard_map/ppermute | solution.py:13
  71.7 232.3 %collective-permute-start.3 = (bf16[2,6,1024,128]{2,3,1,0:T(8,128)(2,1)}, bf16[2,6,1024,128]{2,3,1,0:T(8,128)(2,1)}, u32[]{:S(2)}, u32[]{:S(2)}) collective-permute-start(bf16[2,6,1024,128]{2,3,1,0:T(8,128)(2,1)} %maximum_bitcast_fusion), channel_id=1, source_target_pairs={{16,0},{24,8},{32,16},{40,24},{48,32},{56,40},{64,48},{72,56},{80,... | collective-permute-start | bytes 9437192 | tf_op jit(solution)/shard_map/ppermute | solution.py:13
  308.0 20.8 %copy-start.1 = (bf16[8,6,128,128]{2,3,1,0:T(8,128)(2,1)S(1)}, bf16[8,6,128,128]{2,3,1,0:T(8,128)(2,1)}, u32[]{:S(2)}) copy-start(bf16[8,6,128,128]{2,3,1,0:T(8,128)(2,1)} %custom-call.3) | copy-start | bytes 4718596
  308.0 20.8 %copy-start.3 = (s32[8]{0:T(128)S(1)}, s32[8]{0:T(128)}, u32[]{:S(2)}) copy-start(s32[8]{0:T(128)} %param.11) | copy-start | bytes 100
  358.6 3.3 copy-start.4
  393.1 3.3 copy-start.4
  427.6 3.3 copy-start.4
  462.1 3.3 copy-start.4
  496.6 3.3 copy-start.4
  531.1 3.3 copy-start.4
  565.6 3.3 copy-start.4
  600.1 3.3 copy-start.4
where the time goes:
time: 626 us; the launch traced here: 624 us
  waiting for transfers between devices  245 us (39%)
  local copies, waits for them, and re-layouts  244 us (39%)
  matrix products  67.5 us (11%)
  loops' own time  21.3 us (3%)
  starting transfers between devices  19.1 us (3%)
  blocking collectives  17.2 us (3%)
  other arithmetic  9.62 us (2%)
    all_to_all x1, waiting for transfers between devices, local(): lax.all_to_all(queries, 'head', split_axis=1, concat_axis=0, tiled=True)  210 us
    gather x8, local copies, waits for them, and re-layouts, one_block(): picked = band_blocks[:, :, positions[block_index]]  86.5 us
    slice x16, local copies, waits for them, and re-layouts, one_block(): picked[0]  58.2 us
    sub x8, matrix products, attend_heads(): scores - row_max  58.1 us
    another operation x1, loops' own time, local(): outputs = lax.map(one_block, jnp.arange(blocks_dev, dtype=jnp.int32))  21.3 us
    while x1, local copies, waits for them, and re-layouts, local(): outputs = lax.map(one_block, jnp.arange(blocks_dev, dtype=jnp.int32))  20.8 us
    slice x8, local copies, waits for them, and re-layouts, one_block(): picked[1]  20.4 us
    all_to_all x1, waiting for transfers between devices, local(): lax.all_to_all(values, 'head', split_axis=1, concat_axis=0, tiled=True)  18.9 us
  transfers between devices with their start and end apart: 7, of which 3 were waited for; matrix products, arithmetic and copies ran while one was open for 5% of the time, Pallas kernels for 0%

commit v1 on v0

v1 whole, which is shorter than its diff:
```python
import functools
import math

import jax
import jax.numpy as jnp
from jax import lax
from jax.experimental import pallas as pl
from jax.experimental.pallas import tpu as pltpu
from jax.sharding import PartitionSpec as P

HD = 128
BLK = 128
KB = 20
SB = 16
HALO = 12
WIN = HALO + SB + HALO
PH = 3
UNROLL = 4
LANES = 128
MESH = pl.DeviceIdType.MESH
EXP2_SCALE = math.log2(math.e) / math.sqrt(HD)


def xor_bit(a, b):
    return a + b - 2 * a * b


def member_device(band, slot):
    y_hi = (band // 2) % 2
    y_lo = xor_bit(slot // 8, y_hi)
    return (band // 4) * 8 + (y_hi * 2 + y_lo) * 2 + band % 2, slot % 8


def attend(block, q_ref, k_ref, v_ref, ones_ref, lists, s_ref):
    query = q_ref[block]
    top = None
    for c in range(KB // 2):
        picked = [k_ref[lists[block, 2 * c + t]] for t in range(2)]
        scores = lax.dot_general(
            query, jnp.concatenate(picked, axis=0), (((1,), (1,)), ((), ())),
            preferred_element_type=jnp.float32,
        )
        s_ref[c] = scores
        top = scores if top is None else jnp.maximum(top, scores)
    top = jnp.max(top, axis=1, keepdims=True) * EXP2_SCALE
    total = None
    for c in range(KB // 2):
        weights = jnp.exp2(s_ref[c] * EXP2_SCALE - top).astype(jnp.bfloat16)
        picked = [
            jnp.concatenate(
                [v_ref[lists[block, 32 + 2 * c + t]], ones_ref[lists[block, 64 + 2 * c + t]]], axis=1
            )
            for t in range(2)
        ]
        part = jnp.dot(weights, jnp.concatenate(picked, axis=0), preferred_element_type=jnp.float32)
        total = part if total is None else total + part
    return (total[:, :HD] / total[:, HD:]).astype(jnp.bfloat16)


def kernel(*refs):
    q_in, k_in, v_in, lists_in, out = refs[:5]
    q, k, v = refs[5:8], refs[8:11], refs[11:14]
    ones_ref, staged, lists_v, lists_s = refs[14:18]
    scores = refs[18 : 18 + UNROLL]
    (q_send, k_send, v_send, l_send, q_recv, k_recv, v_recv, l_recv, l_sem,
     kf_send, vf_send, kf_recv, vf_recv, o_send, o_recv) = refs[18 + UNROLL :]

    seq, head = lax.axis_index("seq"), lax.axis_index("head")
    bands = lax.axis_size("seq") // 2
    y_hi, y_lo, core = (seq // 4) % 2, (seq // 2) % 2, seq % 2
    half = xor_bit(y_lo, y_hi)
    my_band = (seq // 8) * 4 + y_hi * 2 + core
    my_slot = half * 8 + head
    own_band = seq // 2
    own_block = core * 8 + head
    to_self = own_band == my_band
    neighbours = {
        side: member_device((my_band + side + bands) % bands, my_slot) for side in (-1, 1)
    }

    ones_ref[0] = jnp.ones((BLK, HD), jnp.bfloat16)
    ones_ref[1] = jnp.zeros((BLK, HD), jnp.bfloat16)
    for h in range(PH):
        v[h][WIN] = jnp.zeros((BLK, HD), jnp.bfloat16)

    bits = [own_block % 2, (own_block // 2) % 2, (own_block // 4) % 2, own_block // 8]

    def slot_at(step):
        return sum(
            (1 - bit if step >> b & 1 else bit) * (1 << b) for b, bit in enumerate(bits)
        )

    barrier = pltpu.get_barrier_semaphore()

    def greet(device):
        pl.semaphore_signal(barrier, inc=1, device_id=device, device_id_type=MESH)

    def not_me(device):
        return jnp.logical_or(device[0] != seq, device[1] != head)

    for side in (-1, 1):
        greet(neighbours[side])
    for n in range(SB):
        for device in (
            member_device(own_band, slot_at(n)),
            (2 * my_band + n // 8, jnp.int32(n % 8)),
        ):
            pl.when(not_me(device))(functools.partial(greet, device))

    @pl.when(to_self)
    def _():
        pl.semaphore_wait(barrier, 2 * SB)

    @pl.when(jnp.logical_not(to_self))
    def _():
        pl.semaphore_wait(barrier, 2 * SB + 2)

    def push(src, dst, send, recv, device):
        @pl.when(not_me(device))
        def _():
            pltpu.make_async_remote_copy(
                src_ref=src, dst_ref=dst, send_sem=send, recv_sem=recv,
                device_id=device, device_id_type=MESH,
            ).start()

        @pl.when(jnp.logical_not(not_me(device)))
        def _():
            pltpu.make_async_copy(src, dst, recv).start()

    def columns(slot, h):
        return pl.ds(pl.multiple_of((slot * PH + h) * HD, HD), HD)

    def scatter_lists():
        for n in (0, 8):
            push(lists_in, lists_v.at[pl.ds(pl.multiple_of(core * 8, 8), 8)], l_send,
                 l_recv.at[core], member_device(own_band, slot_at(n)))

    def scatter(h):
        for n in range(SB):
            slot = slot_at(n)
            device = member_device(own_band, slot)
            cols, group = columns(slot, h), own_block // 4
            push(k_in.at[:, cols], k[h].at[HALO + own_block], k_send, k_recv.at[h, group], device)
            push(v_in.at[:, cols], v[h].at[HALO + own_block], v_send, v_recv.at[h, group], device)
        for n in range(SB):
            slot = slot_at(n)
            device = member_device(own_band, slot)
            push(q_in.at[:, columns(slot, h)], q[h].at[own_block], q_send, q_recv.at[h], device)

    def arrived(ref, sem):
        pltpu.make_async_copy(ref, ref, sem).wait()

    def forward(h, step):
        group = 2 * xor_bit(half, step // 2) + xor_bit(head // 4, step % 2)
        own = pl.ds(HALO + group * 4, 4)
        for buf, own_sem, send, recv in (
            (k[h], k_recv, kf_send, kf_recv), (v[h], v_recv, vf_send, vf_recv)
        ):
            arrived(buf.at[own], own_sem.at[h, group])

            @pl.when(group >= 1)
            def _():
                pltpu.make_async_remote_copy(
                    src_ref=buf.at[own], dst_ref=buf.at[pl.ds(group * 4 - 4, 4)],
                    send_sem=send.at[h], recv_sem=recv.at[h, 0],
                    device_id=neighbours[1], device_id_type=MESH,
                ).start()

            @pl.when(group <= 2)
            def _():
                pltpu.make_async_remote_copy(
                    src_ref=buf.at[own], dst_ref=buf.at[pl.ds(HALO + SB + group * 4, 4)],
                    send_sem=send.at[h], recv_sem=recv.at[h, 1],
                    device_id=neighbours[-1], device_id_type=MESH,
                ).start()

    scatter_lists()
    scatter(0)
    scatter(1)
    for band in range(2):
        arrived(lists_v.at[pl.ds(band * 8, 8)], l_recv.at[band])
    move = pltpu.make_async_copy(lists_v, lists_s, l_sem)
    move.start()
    move.wait()
    for step in range(4):
        forward(0, step)
    scatter(2)

    for h in range(PH):
        arrived(q[h], q_recv.at[h])
        for side, start in ((0, 0), (1, HALO + SB)):
            arrived(k[h].at[pl.ds(start, HALO)], kf_recv.at[h, side])
            arrived(v[h].at[pl.ds(start, HALO)], vf_recv.at[h, side])

        @pl.loop(0, SB // UNROLL)
        def _(step):
            if h + 1 < PH:
                forward(h + 1, step)
            for u in range(UNROLL):
                block = step * UNROLL + u
                staged[h, block] = attend(block, q[h], k[h], v[h], ones_ref, lists_s, scores[u])
            for u in range(UNROLL):
                block = step * UNROLL + u
                push(staged.at[h, block], out.at[:, columns(my_slot, h)], o_send, o_recv,
                     (2 * my_band + block // 8, block % 8))

    arrived(out, o_recv)
    sent = (
        (k_in, k_send), (v_in, v_send), (q_in, q_send),
    )

    @pl.when(to_self)
    def _():
        some = pl.ds(0, (SB - 1) * PH * HD)
        for ref, sem in sent:
            arrived(ref.at[:, some], sem)
        arrived(staged.at[:, pl.ds(0, SB - 1)], o_send)
        arrived(lists_v.at[pl.ds(0, 8)], l_send)

    @pl.when(jnp.logical_not(to_self))
    def _():
        for ref, sem in sent:
            arrived(ref, sem)
        arrived(staged, o_send)
        arrived(lists_v, l_send)

    for h in range(PH):
        arrived(k[h].at[pl.ds(0, 2 * HALO)], kf_send.at[h])
        arrived(v[h].at[pl.ds(0, 2 * HALO)], vf_send.at[h])


def local(queries, keys, values, block_lists, live_counts):
    seq = lax.axis_index("seq")
    blocks = lax.axis_size("seq") * block_lists.shape[0]
    window = jnp.remainder(block_lists - (seq // 2) * SB + HALO, blocks)
    live = jnp.arange(KB, dtype=jnp.int32)[None, :] < live_counts[:, None]
    k_index = jnp.where(live, window, window[:, :1])
    v_index = jnp.where(live, window, WIN)
    dead = jnp.where(live, 0, 1)
    pad = jnp.zeros((block_lists.shape[0], 32 - KB), jnp.int32)
    lists = jnp.concatenate([k_index, pad, v_index, pad, dead], axis=1)
    lists = jnp.pad(lists, ((0, 0), (0, LANES - lists.shape[1])))
    hbm = pl.BlockSpec(memory_space=pl.ANY)
    dma = pltpu.SemaphoreType.DMA
    bf16 = jnp.bfloat16
    return pl.pallas_call(
        kernel,
        out_shape=jax.ShapeDtypeStruct(queries.shape, bf16),
        in_specs=[hbm] * 4,
        out_specs=hbm,
        scratch_shapes=[pltpu.VMEM((SB, BLK, HD), bf16)] * PH
        + [pltpu.VMEM((WIN, BLK, HD), bf16)] * PH
        + [pltpu.VMEM((WIN + 1, BLK, HD), bf16)] * PH
        + [
            pltpu.VMEM((2, BLK, HD), bf16),
            pltpu.VMEM((PH, SB, BLK, HD), bf16),
            pltpu.VMEM((SB, LANES), jnp.int32),
            pltpu.SMEM((SB, LANES), jnp.int32),
        ]
        + [pltpu.VMEM((KB // 2, BLK, 2 * BLK), jnp.float32)] * UNROLL
        + [dma, dma, dma, dma]
        + [dma((PH,)), dma((PH, 4)), dma((PH, 4)), dma((2,)), dma]
        + [dma((PH,)), dma((PH,)), dma((PH, 2)), dma((PH, 2)), dma, dma],
        compiler_params=pltpu.CompilerParams(
            collective_id=0, has_side_effects=True, vmem_limit_bytes=48 << 20
        ),
    )(queries, keys, values, lists)


def solution(mesh):
    in_specs = (
        P(("seq", "head"), None),
        P(("seq", "head"), None),
        P(("seq", "head"), None),
        P("seq", None),
        P("seq"),
    )
    out_specs = P(("seq", "head"), None)
    return jax.shard_map(local, mesh=mesh, in_specs=in_specs, out_specs=out_specs, check_vma=False)
```

time: 626 us -> 148 us (0.24)
  the two profiles are of different devices: /device:TPU:89 before, /device:TPU:39 now
where the time goes in v1:
time: 148 us; the launch traced here: 147 us
  Pallas kernels  142 us (96%)
  local copies, waits for them, and re-layouts  4.17 us (3%)
  other arithmetic  1.5 us (1%)
    pallas_call x1, Pallas kernels, local(): pl.pallas_call(kernel, out_shape=jax.ShapeDtypeStruct(queries.shape, bf16...  142 us
    unnamed x5, local copies, waits for them, and re-layouts  3.96 us

profile of v1, /device:TPU:39, one launch (start us, length us, event | category | flops | bytes accessed | tf_op | source)
XLA Modules:
  0.0 147.4 jit_solution(158176134929636656)
XLA Ops:
  0.0 0.8 fusion.2
  0.8 0.1 slice_reduce_fusion
  0.9 0.7 fusion.3
  1.6 0.1 concatenate.3
  1.7 0.0 copy-start
  1.7 1.4 copy-done
  3.1 0.0 copy-start.1
  3.1 1.4 copy-done.1
  4.5 141.7 %shard_map.55 = bf16[128,6144]{1,0:T(8,128)(2,1)S(1)} custom-call(bf16[128,6144]{1,0:T(8,128)(2,1)S(1)} %copy-done, bf16[128,6144]{1,0:T(8,128)(2,1)S(1)} %copy-done.1, bf16[128,6144]{1,0:T(8,128)(2,1)} %refs_2_.1, s32[8,128]{1,0:T(8,128)S(1)} %pad.4.refs_3_), custom_call_target="tpu_custom_call" | custom-call | tf_op jit(solution)/shard_map/pallas_call | solution.py:246
  146.3 1.1 copy.7
  (2 shorter events, 0.0 us)
Async XLA Ops:
  1.7 1.4 copy-start
  3.1 1.4 copy-start.1

commit v2 on v1

v2 whole, which is shorter than its diff:
```python
import functools
import math

import jax
import jax.numpy as jnp
from jax import lax
from jax.experimental import pallas as pl
from jax.experimental.pallas import tpu as pltpu
from jax.sharding import PartitionSpec as P

HD = 128
BLK = 128
KB = 20
SB = 16
HALO = 12
WIN = HALO + SB + HALO
PH = 3
UNROLL = 4
LANES = 128
MESH = pl.DeviceIdType.MESH
EXP2_SCALE = math.log2(math.e) / math.sqrt(HD)


def xor_bit(a, b):
    return a + b - 2 * a * b


def device_at(x, y, z, core):
    return (z // 2) * 8 + y * 2 + core, (z % 2) * 4 + x


def attend(block, q_ref, k_ref, v_ref, ones_ref, lists, s_ref):
    query = q_ref[block]
    top = None
    for c in range(KB // 2):
        picked = [k_ref[lists[block, 2 * c + t]] for t in range(2)]
        scores = lax.dot_general(
            query, jnp.concatenate(picked, axis=0), (((1,), (1,)), ((), ())),
            preferred_element_type=jnp.float32,
        )
        s_ref[c] = scores
        top = scores if top is None else jnp.maximum(top, scores)
    top = jnp.max(top, axis=1, keepdims=True) * EXP2_SCALE
    total = None
    for c in range(KB // 2):
        weights = jnp.exp2(s_ref[c] * EXP2_SCALE - top).astype(jnp.bfloat16)
        picked = [
            jnp.concatenate(
                [v_ref[lists[block, 32 + 2 * c + t]], ones_ref[lists[block, 64 + 2 * c + t]]], axis=1
            )
            for t in range(2)
        ]
        part = jnp.dot(weights, jnp.concatenate(picked, axis=0), preferred_element_type=jnp.float32)
        total = part if total is None else total + part
    return (total[:, :HD] / total[:, HD:]).astype(jnp.bfloat16)


def kernel(*refs):
    q_in, k_in, v_in, lists_in, out = refs[:5]
    q, k, v = refs[5:8], refs[8:11], refs[11:14]
    q_pass, k_pass, v_pass = refs[14:17], refs[17:20], refs[20:23]
    ones_ref, staged, lists_v, lists_s = refs[23:27]
    scores = refs[27 : 27 + UNROLL]
    (q_send, k_send, v_send, l_send, q_recv, k_recv, v_recv, l_recv, l_sem,
     qp_recv, kp_recv, vp_recv, qf_send, kf_send, vf_send, kf_recv, vf_recv,
     o_send, o_recv) = refs[27 + UNROLL :]

    seq, head = lax.axis_index("seq"), lax.axis_index("head")
    planes = lax.axis_size("seq") // 4
    y, core, z_lo, x = (seq // 2) % 4, seq % 2, head // 4, head % 4
    z = (seq // 8) * 2 + z_lo
    my_band = 2 * z + core
    my_slot = y * 4 + x
    native = y // 2 == z_lo
    own_core = y % 2
    on_core = own_core == core

    sibling = device_at(x, y, z, 1 - core)
    partner = device_at(x, y, z + 1 - 2 * z_lo, core)
    across = device_at(x, y, (z + 2 * core - 1 + planes) % planes, 1 - core)

    ones_ref[0] = jnp.ones((BLK, HD), jnp.bfloat16)
    ones_ref[1] = jnp.zeros((BLK, HD), jnp.bfloat16)
    for h in range(PH):
        v[h][WIN] = jnp.zeros((BLK, HD), jnp.bfloat16)

    bits = [x % 2, x // 2, y % 2, y // 2]

    def slot_at(step):
        flipped = [1 - bit if step >> b & 1 else bit for b, bit in enumerate(bits)]
        return flipped[0] + 2 * flipped[1], flipped[2] + 2 * flipped[3]

    barrier = pltpu.get_barrier_semaphore()

    def greet(device):
        pl.semaphore_signal(barrier, inc=1, device_id=device, device_id_type=MESH)

    def not_me(device):
        return jnp.logical_or(device[0] != seq, device[1] != head)

    for device in (sibling, partner, across):
        greet(device)
    for n in range(SB):
        for device in (
            device_at(n % 4, n // 4, z, own_core),
            device_at(n % 4, core + 2 * (n // 8), z, (n // 4) % 2),
        ):
            pl.when(not_me(device))(functools.partial(greet, device))
    for n in range(SB // 2):
        greet((2 * my_band + n // 4, (1 - z_lo) * 4 + n % 4))

    @pl.when(jnp.logical_not(native))
    def _():
        for n in range(SB):
            greet(device_at(n % 4, n // 4, z + 1 - 2 * z_lo, own_core))

    off_plane, off_core = xor_bit(y // 2, z_lo), xor_bit(own_core, core)
    pl.semaphore_wait(barrier, 2 * SB + SB // 2 + 1 + SB * off_plane + 2 * off_core)

    def start(src, dst, send, recv, device):
        pltpu.make_async_remote_copy(
            src_ref=src, dst_ref=dst, send_sem=send, recv_sem=recv,
            device_id=device, device_id_type=MESH,
        ).start()

    def push(src, dst, send, recv, device):
        @pl.when(not_me(device))
        def _():
            start(src, dst, send, recv, device)

        @pl.when(jnp.logical_not(not_me(device)))
        def _():
            pltpu.make_async_copy(src, dst, recv).start()

    def columns(slot, h):
        return pl.ds(pl.multiple_of((slot * PH + h) * HD, HD), HD)

    def scatter_lists():
        for n in (0, 4, 8, 12):
            tx, ty = slot_at(n)
            push(lists_in, lists_v.at[pl.ds(pl.multiple_of(core * 8, 8), 8)], l_send,
                 l_recv.at[core], device_at(tx, ty, z, own_core))

    def scatter(h):
        def send_all(names):
            @pl.when(native)
            def _():
                for n in range(SB):
                    tx, ty = slot_at(n)
                    for src, dst, _, send, recv, _, first in names:
                        push(src.at[:, columns(ty * 4 + tx, h)],
                             dst[h].at[first + core * 8 + z_lo * 4 + x], send,
                             recv.at[h, core * 2 + z_lo], device_at(tx, ty, z, own_core))

            @pl.when(jnp.logical_not(native))
            def _():
                for n in range(SB):
                    tx, ty = slot_at(n)
                    for src, _, dst, send, _, recv, _ in names:
                        push(src.at[:, columns(ty * 4 + tx, h)],
                             dst[h].at[core * 4 + x], send,
                             recv.at[h, core], device_at(tx, ty, z, own_core))

        send_all(((k_in, k, k_pass, k_send, k_recv, kp_recv, HALO),
                  (v_in, v, v_pass, v_send, v_recv, vp_recv, HALO)))
        send_all(((q_in, q, q_pass, q_send, q_recv, qp_recv, 0),))

    def arrived(ref, sem):
        pltpu.make_async_copy(ref, ref, sem).wait()

    def four(start_block):
        return pl.ds(start_block, 4)

    def relay(h, part):
        group = part * 2 + z_lo
        src = four(part * 4)
        for buf, passed, pass_recv, send, own_recv, recv in (
            (k[h], k_pass[h], kp_recv, kf_send, k_recv, kf_recv),
            (v[h], v_pass[h], vp_recv, vf_send, v_recv, vf_recv),
        ):
            arrived(passed.at[src], pass_recv.at[h, part])
            start(passed.at[src], buf.at[four(HALO + group * 4)], send.at[h],
                  own_recv.at[h, group], partner)

            @pl.when(jnp.logical_and(core == 1, z_lo == 1))
            def _():
                start(passed.at[src], buf.at[four(part * 8)], send.at[h], recv.at[h, 0], sibling)

            @pl.when(jnp.logical_and(core == 0, z_lo == 0))
            def _():
                start(passed.at[src], buf.at[four(HALO + SB + part * 8)], send.at[h],
                      recv.at[h, 1], sibling)
        arrived(q_pass[h].at[src], qp_recv.at[h, part])
        start(q_pass[h].at[src], q[h].at[four(group * 4)], qf_send.at[h],
              q_recv.at[h, group], partner)

    right = tuple(jnp.where(core == 0, a, b) for a, b in zip(sibling, across))
    left = tuple(jnp.where(core == 0, b, a) for a, b in zip(sibling, across))

    def share(h, which):
        for part in range(2):
            group = part * 2 + xor_bit(z_lo, which)
            own = four(HALO + group * 4)
            to_right = jnp.logical_and(
                group >= 1,
                jnp.logical_or(jnp.logical_or(core == 0, z_lo == 1), group == 2),
            )
            to_left = jnp.logical_and(
                group <= 2,
                jnp.logical_or(jnp.logical_or(core == 1, z_lo == 0), group == 1),
            )
            for buf, own_recv, send, recv in (
                (k[h], k_recv, kf_send, kf_recv), (v[h], v_recv, vf_send, vf_recv)
            ):
                arrived(buf.at[own], own_recv.at[h, group])

                @pl.when(to_right)
                def _():
                    start(buf.at[own], buf.at[four(group * 4 - 4)], send.at[h],
                          recv.at[h, 0], right)

                @pl.when(to_left)
                def _():
                    start(buf.at[own], buf.at[four(HALO + SB + group * 4)], send.at[h],
                          recv.at[h, 1], left)

    def forward(h, step):
        @pl.when(step < 2)
        def _():
            relay(h, step)

        @pl.when(step >= 2)
        def _():
            share(h, step - 2)

    pl.when(native)(scatter_lists)
    scatter(0)
    scatter(1)
    for band in range(2):
        arrived(lists_v.at[pl.ds(band * 8, 8)], l_recv.at[band])
    move = pltpu.make_async_copy(lists_v.at[pl.ds(0, SB)], lists_s, l_sem)
    move.start()
    move.wait()
    for step in range(2):
        relay(0, step)
    scatter(2)
    for step in range(2):
        share(0, step)

    for h in range(PH):
        for group in range(4):
            arrived(q[h].at[four(group * 4)], q_recv.at[h, group])
        for side, first in ((0, 0), (1, HALO + SB)):
            arrived(k[h].at[pl.ds(first, HALO)], kf_recv.at[h, side])
            arrived(v[h].at[pl.ds(first, HALO)], vf_recv.at[h, side])

        @pl.loop(0, SB // UNROLL)
        def _(step):
            if h + 1 < PH:
                forward(h + 1, step)
            for u in range(UNROLL):
                block = step * UNROLL + u
                staged[h, block] = attend(block, q[h], k[h], v[h], ones_ref, lists_s, scores[u])
            for u in range(UNROLL):
                block = step * UNROLL + u
                push(staged.at[h, block], out.at[:, columns(my_slot, h)], o_send, o_recv,
                     (2 * my_band + block // 8, block % 8))

    arrived(out, o_recv)
    sent = ((k_in, k_send), (v_in, v_send), (q_in, q_send))

    @pl.when(on_core)
    def _():
        for ref, sem in sent:
            arrived(ref.at[:, pl.ds(0, (SB - 1) * PH * HD)], sem)

    @pl.when(jnp.logical_not(on_core))
    def _():
        for ref, sem in sent:
            arrived(ref, sem)

    mine = jnp.logical_and(on_core, native)

    @pl.when(mine)
    def _():
        arrived(staged.at[:, pl.ds(0, SB - 1)], o_send)
        arrived(lists_v.at[pl.ds(0, 24)], l_send)

    @pl.when(jnp.logical_not(mine))
    def _():
        arrived(staged, o_send)

    @pl.when(jnp.logical_and(jnp.logical_not(on_core), native))
    def _():
        arrived(lists_v, l_send)

    @pl.when(core == z_lo)
    def _():
        for h in range(PH):
            arrived(k[h], kf_send.at[h])
            arrived(v[h].at[pl.ds(0, WIN)], vf_send.at[h])

    @pl.when(core != z_lo)
    def _():
        for h in range(PH):
            arrived(k[h].at[pl.ds(0, 2 * HALO)], kf_send.at[h])
            arrived(v[h].at[pl.ds(0, 2 * HALO)], vf_send.at[h])

    for h in range(PH):
        arrived(q_pass[h], qf_send.at[h])


def local(queries, keys, values, block_lists, live_counts):
    seq = lax.axis_index("seq")
    blocks = lax.axis_size("seq") * block_lists.shape[0]
    window = jnp.remainder(block_lists - (seq // 2) * SB + HALO, blocks)
    live = jnp.arange(KB, dtype=jnp.int32)[None, :] < live_counts[:, None]
    k_index = jnp.where(live, window, window[:, :1])
    v_index = jnp.where(live, window, WIN)
    dead = jnp.where(live, 0, 1)
    pad = jnp.zeros((block_lists.shape[0], 32 - KB), jnp.int32)
    lists = jnp.concatenate([k_index, pad, v_index, pad, dead], axis=1)
    lists = jnp.pad(lists, ((0, 0), (0, LANES - lists.shape[1])))
    hbm = pl.BlockSpec(memory_space=pl.ANY)
    dma = pltpu.SemaphoreType.DMA
    bf16 = jnp.bfloat16
    return pl.pallas_call(
        kernel,
        out_shape=jax.ShapeDtypeStruct(queries.shape, bf16),
        in_specs=[hbm] * 4,
        out_specs=hbm,
        scratch_shapes=[pltpu.VMEM((SB, BLK, HD), bf16)] * PH
        + [pltpu.VMEM((WIN, BLK, HD), bf16)] * PH
        + [pltpu.VMEM((WIN + 1, BLK, HD), bf16)] * PH
        + [pltpu.VMEM((SB // 2, BLK, HD), bf16)] * (3 * PH)
        + [
            pltpu.VMEM((2, BLK, HD), bf16),
            pltpu.VMEM((PH, SB, BLK, HD), bf16),
            pltpu.VMEM((2 * SB, LANES), jnp.int32),
            pltpu.SMEM((SB, LANES), jnp.int32),
        ]
        + [pltpu.VMEM((KB // 2, BLK, 2 * BLK), jnp.float32)] * UNROLL
        + [dma, dma, dma, dma]
        + [dma((PH, 4)), dma((PH, 4)), dma((PH, 4)), dma((2,)), dma]
        + [dma((PH, 2)), dma((PH, 2)), dma((PH, 2))]
        + [dma((PH,)), dma((PH,)), dma((PH,)), dma((PH, 2)), dma((PH, 2)), dma, dma],
        compiler_params=pltpu.CompilerParams(
            collective_id=0, has_side_effects=True, vmem_limit_bytes=48 << 20
        ),
    )(queries, keys, values, lists)


def solution(mesh):
    in_specs = (
        P(("seq", "head"), None),
        P(("seq", "head"), None),
        P(("seq", "head"), None),
        P("seq", None),
        P("seq"),
    )
    out_specs = P(("seq", "head"), None)
    return jax.shard_map(local, mesh=mesh, in_specs=in_specs, out_specs=out_specs, check_vma=False)
```

time: 148 us -> 119 us (0.80)
  the two profiles are of different devices: /device:TPU:39 before, /device:TPU:41 now
where the time goes in v2:
time: 119 us
  Pallas kernels  113 us (95%)
  local copies, waits for them, and re-layouts  4.17 us (4%)
  other arithmetic  1.5 us (1%)
    pallas_call x1, Pallas kernels, local(): pl.pallas_call(kernel, out_shape=jax.ShapeDtypeStruct(queries.shape, bf16...  113 us
    unnamed x5, local copies, waits for them, and re-layouts  3.96 us

profile of v2, /device:TPU:41, one launch (start us, length us, event | category | flops | bytes accessed | tf_op | source)
XLA Modules:
  0.0 118.8 jit_solution(11922177732178893760)
XLA Ops:
  0.0 0.8 fusion.2
  0.8 0.1 slice_reduce_fusion
  0.9 0.7 fusion.3
  1.6 0.1 concatenate.3
  1.7 0.0 copy-start
  1.7 1.4 %copy-done = bf16[128,6144]{1,0:T(8,128)(2,1)S(1)} copy-done((bf16[128,6144]{1,0:T(8,128)(2,1)S(1)}, bf16[128,6144]{1,0:T(8,128)(2,1)}, u32[]{:S(2)}) %copy-start) | copy-done | bytes 1572888
  3.1 0.0 copy-start.1
  3.1 1.4 %copy-done.1 = bf16[128,6144]{1,0:T(8,128)(2,1)S(1)} copy-done((bf16[128,6144]{1,0:T(8,128)(2,1)S(1)}, bf16[128,6144]{1,0:T(8,128)(2,1)}, u32[]{:S(2)}) %copy-start.1) | copy-done | bytes 1572888
  4.5 113.1 %shard_map.55 = bf16[128,6144]{1,0:T(8,128)(2,1)S(1)} custom-call(bf16[128,6144]{1,0:T(8,128)(2,1)S(1)} %copy-done, bf16[128,6144]{1,0:T(8,128)(2,1)S(1)} %copy-done.1, bf16[128,6144]{1,0:T(8,128)(2,1)} %refs_2_.1, s32[8,128]{1,0:T(8,128)S(1)} %pad.4.refs_3_), custom_call_target="tpu_custom_call" | custom-call | tf_op jit(solution)/shard_map/pallas_call | solution.py:327
  117.7 1.1 copy.7
  (2 shorter events, 0.0 us)
Async XLA Ops:
  1.7 1.4 %copy-start = (bf16[128,6144]{1,0:T(8,128)(2,1)S(1)}, bf16[128,6144]{1,0:T(8,128)(2,1)}, u32[]{:S(2)}) copy-start(bf16[128,6144]{1,0:T(8,128)(2,1)} %refs_0_.1) | copy-start | bytes 4718596
  3.1 1.4 %copy-start.1 = (bf16[128,6144]{1,0:T(8,128)(2,1)S(1)}, bf16[128,6144]{1,0:T(8,128)(2,1)}, u32[]{:S(2)}) copy-start(bf16[128,6144]{1,0:T(8,128)(2,1)} %refs_1_.1) | copy-start | bytes 4718596

commit v3 on v2

--- a/solution.py
+++ b/solution.py
@@ -56,17 +56,18 @@
 
 
 def kernel(*refs):
-    q_in, k_in, v_in, lists_in, out = refs[:5]
-    q, k, v = refs[5:8], refs[8:11], refs[11:14]
-    q_pass, k_pass, v_pass = refs[14:17], refs[17:20], refs[20:23]
-    ones_ref, staged, lists_v, lists_s = refs[23:27]
-    scores = refs[27 : 27 + UNROLL]
+    q_in, k_in, v_in, listed_in, live_in, out = refs[:6]
+    q, k, v = refs[6:9], refs[9:12], refs[12:15]
+    q_pass, k_pass, v_pass = refs[15:18], refs[18:21], refs[21:24]
+    ones_ref, staged, lists_v, lists_s, listed, live, own_lists = refs[24:31]
+    scores = refs[31 : 31 + UNROLL]
     (q_send, k_send, v_send, l_send, q_recv, k_recv, v_recv, l_recv, l_sem,
      qp_recv, kp_recv, vp_recv, qf_send, kf_send, vf_send, kf_recv, vf_recv,
-     o_send, o_recv) = refs[27 + UNROLL :]
+     o_send, o_recv, in_sem) = refs[31 + UNROLL :]
 
     seq, head = lax.axis_index("seq"), lax.axis_index("head")
     planes = lax.axis_size("seq") // 4
+    bands = lax.axis_size("seq") // 2
     y, core, z_lo, x = (seq // 2) % 4, seq % 2, head // 4, head % 4
     z = (seq // 8) * 2 + z_lo
     my_band = 2 * z + core
@@ -79,6 +80,12 @@
     partner = device_at(x, y, z + 1 - 2 * z_lo, core)
     across = device_at(x, y, (z + 2 * core - 1 + planes) % planes, 1 - core)
 
+    inputs = (
+        pltpu.make_async_copy(listed_in, listed, in_sem.at[0]),
+        pltpu.make_async_copy(live_in, live, in_sem.at[1]),
+    )
+    for copy in inputs:
+        copy.start()
     ones_ref[0] = jnp.ones((BLK, HD), jnp.bfloat16)
     ones_ref[1] = jnp.zeros((BLK, HD), jnp.bfloat16)
     for h in range(PH):
@@ -135,35 +142,51 @@
     def columns(slot, h):
         return pl.ds(pl.multiple_of((slot * PH + h) * HD, HD), HD)
 
+    def make_lists():
+        for copy in inputs:
+            copy.wait()
+        blocks = bands * SB
+        row = lax.broadcasted_iota(jnp.int32, listed.shape, 0)
+        counted = sum(jnp.where(row == r, live[r], 0) for r in range(listed.shape[0]))
+        counts = lax.broadcasted_iota(jnp.int32, listed.shape, 1) < counted
+        own_band = (z // 2) * 4 + y
+        window = listed[...] - own_band * SB + HALO
+        window = jnp.where(window < 0, window + blocks, window)
+        window = jnp.where(window >= blocks, window - blocks, window)
+        own_lists[...] = jnp.zeros_like(own_lists)
+        own_lists[:, 0:KB] = jnp.where(counts, window, row + (HALO + core * 8))
+        own_lists[:, 32 : 32 + KB] = jnp.where(counts, window, WIN)
+        own_lists[:, 64 : 64 + KB] = jnp.where(counts, 0, 1)
+
     def scatter_lists():
         for n in (0, 4, 8, 12):
             tx, ty = slot_at(n)
-            push(lists_in, lists_v.at[pl.ds(pl.multiple_of(core * 8, 8), 8)], l_send,
+            push(own_lists, lists_v.at[pl.ds(pl.multiple_of(core * 8, 8), 8)], l_send,
                  l_recv.at[core], device_at(tx, ty, z, own_core))
 
     def scatter(h):
         def send_all(names):
             @pl.when(native)
             def _():
-                for n in range(SB):
-                    tx, ty = slot_at(n)
-                    for src, dst, _, send, recv, _, first in names:
+                for src, dst, _, send, recv, _, first in names:
+                    for n in range(SB):
+                        tx, ty = slot_at(n)
                         push(src.at[:, columns(ty * 4 + tx, h)],
                              dst[h].at[first + core * 8 + z_lo * 4 + x], send,
                              recv.at[h, core * 2 + z_lo], device_at(tx, ty, z, own_core))
 
             @pl.when(jnp.logical_not(native))
             def _():
-                for n in range(SB):
-                    tx, ty = slot_at(n)
-                    for src, _, dst, send, _, recv, _ in names:
+                for src, _, dst, send, _, recv, _ in names:
+                    for n in range(SB):
+                        tx, ty = slot_at(n)
                         push(src.at[:, columns(ty * 4 + tx, h)],
                              dst[h].at[core * 4 + x], send,
                              recv.at[h, core], device_at(tx, ty, z, own_core))
 
         send_all(((k_in, k, k_pass, k_send, k_recv, kp_recv, HALO),
-                  (v_in, v, v_pass, v_send, v_recv, vp_recv, HALO)))
-        send_all(((q_in, q, q_pass, q_send, q_recv, qp_recv, 0),))
+                  (v_in, v, v_pass, v_send, v_recv, vp_recv, HALO),
+                  (q_in, q, q_pass, q_send, q_recv, qp_recv, 0)))
 
     def arrived(ref, sem):
         pltpu.make_async_copy(ref, ref, sem).wait()
@@ -171,13 +194,14 @@
     def four(start_block):
         return pl.ds(start_block, 4)
 
-    def relay(h, part):
-        group = part * 2 + z_lo
-        src = four(part * 4)
-        for buf, passed, pass_recv, send, own_recv, recv in (
-            (k[h], k_pass[h], kp_recv, kf_send, k_recv, kf_recv),
-            (v[h], v_pass[h], vp_recv, vf_send, v_recv, vf_recv),
-        ):
+    keys = (k, k_pass, kp_recv, kf_send, k_recv, kf_recv)
+    values = (v, v_pass, vp_recv, vf_send, v_recv, vf_recv)
+
+    def relay(h, names):
+        bufs, passes, pass_recv, send, own_recv, recv = names
+        buf, passed = bufs[h], passes[h]
+        for part in range(2):
+            group, src = part * 2 + z_lo, four(part * 4)
             arrived(passed.at[src], pass_recv.at[h, part])
             start(passed.at[src], buf.at[four(HALO + group * 4)], send.at[h],
                   own_recv.at[h, group], partner)
@@ -190,14 +214,20 @@
             def _():
                 start(passed.at[src], buf.at[four(HALO + SB + part * 8)], send.at[h],
                       recv.at[h, 1], sibling)
-        arrived(q_pass[h].at[src], qp_recv.at[h, part])
-        start(q_pass[h].at[src], q[h].at[four(group * 4)], qf_send.at[h],
-              q_recv.at[h, group], partner)
+
+    def relay_queries(h):
+        for part in range(2):
+            group, src = part * 2 + z_lo, four(part * 4)
+            arrived(q_pass[h].at[src], qp_recv.at[h, part])
+            start(q_pass[h].at[src], q[h].at[four(group * 4)], qf_send.at[h],
+                  q_recv.at[h, group], partner)
 
     right = tuple(jnp.where(core == 0, a, b) for a, b in zip(sibling, across))
     left = tuple(jnp.where(core == 0, b, a) for a, b in zip(sibling, across))
 
-    def share(h, which):
+    def share(h, which, names):
+        bufs, _, _, send, own_recv, recv = names
+        buf = bufs[h]
         for part in range(2):
             group = part * 2 + xor_bit(z_lo, which)
             own = four(HALO + group * 4)
@@ -209,45 +239,45 @@
                 group <= 2,
                 jnp.logical_or(jnp.logical_or(core == 1, z_lo == 0), group == 1),
             )
-            for buf, own_recv, send, recv in (
-                (k[h], k_recv, kf_send, kf_recv), (v[h], v_recv, vf_send, vf_recv)
-            ):
-                arrived(buf.at[own], own_recv.at[h, group])
-
-                @pl.when(to_right)
-                def _():
-                    start(buf.at[own], buf.at[four(group * 4 - 4)], send.at[h],
-                          recv.at[h, 0], right)
-
-                @pl.when(to_left)
-                def _():
-                    start(buf.at[own], buf.at[four(HALO + SB + group * 4)], send.at[h],
-                          recv.at[h, 1], left)
-
-    def forward(h, step):
-        @pl.when(step < 2)
-        def _():
-            relay(h, step)
-
-        @pl.when(step >= 2)
-        def _():
-            share(h, step - 2)
-
+            arrived(buf.at[own], own_recv.at[h, group])
+
+            @pl.when(to_right)
+            def _():
+                start(buf.at[own], buf.at[four(group * 4 - 4)], send.at[h], recv.at[h, 0], right)
+
+            @pl.when(to_left)
+            def _():
+                start(buf.at[own], buf.at[four(HALO + SB + group * 4)], send.at[h],
+                      recv.at[h, 1], left)
+
+    def early(h):
+        for names in (keys, values):
+            relay(h, names)
+            share(h, 0, names)
+
+    def late(h, step):
+        if step == 0:
+            relay_queries(h)
+        else:
+            share(h, 1, (keys, values)[step - 1])
+
+    scatter(0)
+    make_lists()
     pl.when(native)(scatter_lists)
-    scatter(0)
     scatter(1)
+    early(0)
+    scatter(2)
+    for step in range(3):
+        late(0, step)
     for band in range(2):
         arrived(lists_v.at[pl.ds(band * 8, 8)], l_recv.at[band])
     move = pltpu.make_async_copy(lists_v.at[pl.ds(0, SB)], lists_s, l_sem)
     move.start()
     move.wait()
-    for step in range(2):
-        relay(0, step)
-    scatter(2)
-    for step in range(2):
-        share(0, step)
 
     for h in range(PH):
+        if h + 1 < PH:
+            early(h + 1)
         for group in range(4):
             arrived(q[h].at[four(group * 4)], q_recv.at[h, group])
         for side, first in ((0, 0), (1, HALO + SB)):
@@ -257,7 +287,8 @@
         @pl.loop(0, SB // UNROLL)
         def _(step):
             if h + 1 < PH:
-                forward(h + 1, step)
+                for n in range(3):
+                    pl.when(step == n)(functools.partial(late, h + 1, n))
             for u in range(UNROLL):
                 block = step * UNROLL + u
                 staged[h, block] = attend(block, q[h], k[h], v[h], ones_ref, lists_s, scores[u])
@@ -311,23 +342,13 @@
 
 
 def local(queries, keys, values, block_lists, live_counts):
-    seq = lax.axis_index("seq")
-    blocks = lax.axis_size("seq") * block_lists.shape[0]
-    window = jnp.remainder(block_lists - (seq // 2) * SB + HALO, blocks)
-    live = jnp.arange(KB, dtype=jnp.int32)[None, :] < live_counts[:, None]
-    k_index = jnp.where(live, window, window[:, :1])
-    v_index = jnp.where(live, window, WIN)
-    dead = jnp.where(live, 0, 1)
-    pad = jnp.zeros((block_lists.shape[0], 32 - KB), jnp.int32)
-    lists = jnp.concatenate([k_index, pad, v_index, pad, dead], axis=1)
-    lists = jnp.pad(lists, ((0, 0), (0, LANES - lists.shape[1])))
     hbm = pl.BlockSpec(memory_space=pl.ANY)
     dma = pltpu.SemaphoreType.DMA
     bf16 = jnp.bfloat16
     return pl.pallas_call(
         kernel,
         out_shape=jax.ShapeDtypeStruct(queries.shape, bf16),
-        in_specs=[hbm] * 4,
+        in_specs=[hbm] * 5,
         out_specs=hbm,
         scratch_shapes=[pltpu.VMEM((SB, BLK, HD), bf16)] * PH
         + [pltpu.VMEM((WIN, BLK, HD), bf16)] * PH
@@ -338,16 +359,19 @@
             pltpu.VMEM((PH, SB, BLK, HD), bf16),
             pltpu.VMEM((2 * SB, LANES), jnp.int32),
             pltpu.SMEM((SB, LANES), jnp.int32),
+            pltpu.VMEM(block_lists.shape, jnp.int32),
+            pltpu.SMEM(live_counts.shape, jnp.int32),
+            pltpu.VMEM((block_lists.shape[0], LANES), jnp.int32),
         ]
         + [pltpu.VMEM((KB // 2, BLK, 2 * BLK), jnp.float32)] * UNROLL
         + [dma, dma, dma, dma]
         + [dma((PH, 4)), dma((PH, 4)), dma((PH, 4)), dma((2,)), dma]
         + [dma((PH, 2)), dma((PH, 2)), dma((PH, 2))]
-        + [dma((PH,)), dma((PH,)), dma((PH,)), dma((PH, 2)), dma((PH, 2)), dma, dma],
+        + [dma((PH,)), dma((PH,)), dma((PH,)), dma((PH, 2)), dma((PH, 2)), dma, dma, dma((2,))],
         compiler_params=pltpu.CompilerParams(
-            collective_id=0, has_side_effects=True, vmem_limit_bytes=48 << 20
+            collective_id=0, has_side_effects=True, vmem_limit_bytes=62 << 20
         ),
-    )(queries, keys, values, lists)
+    )(queries, keys, values, block_lists, live_counts)
 
 
 def solution(mesh):

time: 119 us -> 106 us (0.89)
  the two profiles are of different devices: /device:TPU:41 before, /device:TPU:225 now
where the time goes in v3:
time: 106 us
  Pallas kernels  103 us (97%)
  local copies, waits for them, and re-layouts  2.69 us (3%)
    pallas_call x1, Pallas kernels, local(): pl.pallas_call(kernel, out_shape=jax.ShapeDtypeStruct(queries.shape, bf16...  103 us
    unnamed x1, local copies, waits for them, and re-layouts  2.69 us

profile of v3, /device:TPU:225, one launch (start us, length us, event | category | flops | bytes accessed | tf_op | source)
XLA Modules:
  0.0 105.6 jit_solution(11225061105030972260)
XLA Ops:
  0.0 102.9 %shard_map.55 = bf16[128,6144]{1,0:T(8,128)(2,1)} custom-call(bf16[128,6144]{1,0:T(8,128)(2,1)} %refs_0_.1, bf16[128,6144]{1,0:T(8,128)(2,1)} %refs_1_.1, bf16[128,6144]{1,0:T(8,128)(2,1)} %refs_2_.1, s32[8,20]{1,0:T(8,128)} %refs_3_.1, s32[8]{0:T(128)} %refs_4_.1), custom_call_target="tpu_custom_call" | custom-call | tf_op jit(solution)/shard_map/pallas_call | solution.py:348
  102.9 2.7 %copy.7 = bf16[128,6144]{1,0:T(8,128)(2,1)} copy(bf16[128,6144]{1,0:T(8,128)(2,1)} %shard_map.55) | data formatting | bytes 3145728
